TPU v7x, 512 devices: a whole 4x8x8 slice. The times are simulated.
512 devices in a mesh: streams: 16 (over y, core), tp: 32 (over x, z).
Axes of the slice: x: 4, y: 8, z: 8, core: 2. Of those that a mesh axis runs over, the one named last changes fastest.
Arguments:
- hidden_in: bfloat16 [512, 4, 1024], P(('streams', 'tp')), may hold values from -6 to 6
- byte_qkv: bfloat16 [512, 4, 1536], P(('streams', 'tp'))
- byte_cache: bfloat16 [512, 256, 512], P(('streams', 'tp'))
- byte_len: int32 [512], P(('streams', 'tp')), may hold values from 2 to 256, as said below
- flags: int32 [512, 4], P(('streams', 'tp')), may hold values 0 or 1
- coarse_prev: bfloat16 [512, 1024], P(('streams', 'tp')), may hold values from -6 to 6
- owner_map: int32 [32, 16, 1], replicated, may hold values from 0 to 15; in each aligned block of 16 rows (0 to 15, 16 to 31, ..., all dimensions but the last counted through in order) at most 2 rows name the same one
- up_weight: bfloat16 [1024, 8192], P(None, 'tp'), may hold values from -0.1875 to 0.1875
- coarse_gain: float32 [8192], replicated, may hold values from 0.5 to 1.5
- query_weight: bfloat16 [8192, 4096], P(None, 'tp'), may hold values from -0.0625 to 0.0625
- keyval_weight: bfloat16 [8192, 1024], P('tp'), may hold values from -0.0625 to 0.0625
- return_weight: bfloat16 [4096, 1024], P('tp'), may hold values from -0.09375 to 0.09375
- coarse_cache: bfloat16 [16, 64, 32, 32, 256], P('streams', None, 'tp'), as said below
- coarse_len: int32 [16, 64], P('streams'), may hold values from 1 to 32, as said below
Outputs:
- byte_out: bfloat16 [512, 4, 1024], P(('streams', 'tp'))
Inputs may be any that keep to these rules, and one draw needn't show every extreme that they name: `owner_map`: within one index c of tp, no group owns more than 2 of the sequences s * 32 + c, and some group owns exactly 2. `byte_len`: some sequence has exactly 256 filled positions. `coarse_len`: some slot has exactly 32 filled positions. `coarse_cache`: the copies for heads h and h2 are equal where h // 8 = h2 // 8.
All inputs are finite; a program needn't handle non-finite values. No bound on the sum of `flags` on one device may be relied on, other than what follows from the above.
Results may differ from a plain program's by a relative error of at most 0.014.
Values may be sent and summed in bfloat16 or wider, within the bound.
A program may use at most 64 MiB of HBM per device.

v0:
```python
import jax
import jax.numpy as jnp
from jax import lax
from jax.sharding import PartitionSpec as P

HD = 128
OWNED_MOST = 2
EPSILON = 1e-05
NEG_FILL = -1e30


def split_softmax(scores_old, scores_new):
    largest = jnp.maximum(
        jnp.max(scores_old, axis=-1, keepdims=True), jnp.max(scores_new, axis=-1, keepdims=True)
    )
    exp_old = jnp.exp(scores_old - largest)
    exp_new = jnp.exp(scores_new - largest)
    denominator = jnp.sum(exp_old, axis=-1, keepdims=True) + jnp.sum(
        exp_new, axis=-1, keepdims=True
    )
    return (
        (exp_old / denominator).astype(jnp.bfloat16),
        (exp_new / denominator).astype(jnp.bfloat16),
    )


def rank_table(owner_map):
    owners = owner_map[:, :, 0]
    group_total = owners.shape[1]
    same_owner = owners[:, :, None] == owners[:, None, :]
    earlier = (
        jnp.arange(group_total, dtype=jnp.int32)[None, :, None]
        > jnp.arange(group_total, dtype=jnp.int32)[None, None, :]
    )
    ranking = jnp.sum((same_owner & earlier).astype(jnp.int32), axis=2)
    return (owners, ranking)


def byte_attention(byte_qkv, byte_cache, byte_len):
    number, step_count, total_width = byte_qkv.shape
    length = byte_cache.shape[1]
    kv_width = byte_cache.shape[2] // 2
    kv_groups = kv_width // HD
    head_count = (total_width - 2 * kv_width) // HD
    group_size = head_count // kv_groups
    query_part = byte_qkv[:, :, : head_count * HD].reshape(
        number, step_count, kv_groups, group_size, HD
    )
    new_keys = byte_qkv[:, :, head_count * HD : head_count * HD + kv_width].reshape(
        number, step_count, kv_groups, HD
    )
    new_values = byte_qkv[:, :, head_count * HD + kv_width :].reshape(
        number, step_count, kv_groups, HD
    )
    old_keys = byte_cache[:, :, :kv_width].reshape(number, length, kv_groups, HD)
    old_values = byte_cache[:, :, kv_width:].reshape(number, length, kv_groups, HD)
    scaling = HD ** (-0.5)
    scores_old = (
        jnp.einsum("nsgjd,nlgd->nsgjl", query_part, old_keys, preferred_element_type=jnp.float32)
        * scaling
    )
    valid_old = jnp.arange(length, dtype=jnp.int32)[None, :] < byte_len[:, None]
    scores_old = jnp.where(valid_old[:, None, None, None, :], scores_old, NEG_FILL)
    scores_new = (
        jnp.einsum("nsgjd,nugd->nsgju", query_part, new_keys, preferred_element_type=jnp.float32)
        * scaling
    )
    causal = jnp.arange(step_count)[:, None] >= jnp.arange(step_count)[None, :]
    scores_new = jnp.where(causal[None, :, None, None, :], scores_new, NEG_FILL)
    weights_old, weights_new = split_softmax(scores_old, scores_new)
    mixed_heads = jnp.einsum(
        "nsgjl,nlgd->nsgjd", weights_old, old_values, preferred_element_type=jnp.float32
    )
    mixed_heads = mixed_heads + jnp.einsum(
        "nsgju,nugd->nsgjd", weights_new, new_values, preferred_element_type=jnp.float32
    )
    return mixed_heads.reshape(number, step_count, head_count * HD)


def dispatch(block_rows, block_marks, owners, ranking):
    column_total = lax.axis_size("tp")
    row_index = lax.axis_index("streams")
    every_rows, every_marks = (
        lax.all_gather(block_rows, ("streams", "tp"), axis=0, tiled=True),
        lax.all_gather(block_marks, ("streams", "tp"), axis=0, tiled=True),
    )
    target = jnp.where(
        owners == row_index,
        jnp.arange(column_total, dtype=jnp.int32)[:, None] * OWNED_MOST + ranking,
        -1,
    )
    target_flat = target.T.reshape(-1)
    slot_ids = jnp.arange(column_total * OWNED_MOST, dtype=jnp.int32)
    picker = (slot_ids[:, None] == target_flat[None, :]).astype(jnp.bfloat16)
    slot_rows = jnp.einsum(
        "ai,ibd->abd", picker, every_rows, preferred_element_type=jnp.float32
    ).astype(jnp.bfloat16)
    slot_marks = jnp.einsum("ai,ib->ab", picker, every_marks, preferred_element_type=jnp.float32)
    return (slot_rows, slot_marks)


def coarse_project(slot_rows, up_weight, coarse_gain, query_weight, keyval_weight):
    column_total = lax.axis_size("tp")
    column = lax.axis_index("tp")
    part_width = up_weight.shape[1]
    expanded = jnp.einsum(
        "rbd,df->rbf", slot_rows, up_weight, preferred_element_type=jnp.float32
    ).astype(jnp.bfloat16)
    widened = lax.all_gather(expanded, "tp", axis=2, tiled=True).astype(jnp.float32)
    scaled_part = (widened * coarse_gain).astype(jnp.bfloat16)
    query_sum = jnp.einsum(
        "rbf,fh->rbh", scaled_part, query_weight, preferred_element_type=jnp.float32
    )
    squares = jnp.sum(widened * widened, axis=2)
    query_sum, squares = (query_sum, squares)
    own_gains = lax.dynamic_slice_in_dim(coarse_gain, column * part_width, part_width, 0)
    own_scaled = (expanded.astype(jnp.float32) * own_gains).astype(jnp.bfloat16)
    inverse = lax.rsqrt(squares / (part_width * column_total) + EPSILON)[:, :, None]
    queries = (query_sum * inverse).astype(jnp.bfloat16)
    kv_width = keyval_weight.shape[1]
    kv_heads = kv_width // (2 * HD)
    group_size = column_total // kv_heads
    head_group = column // group_size
    keyval_part = jnp.einsum(
        "rbf,fc->rbc", own_scaled, keyval_weight, preferred_element_type=jnp.float32
    )
    keyvals = lax.psum(keyval_part, "tp")
    new_keys = (lax.dynamic_slice_in_dim(keyvals, head_group * HD, HD, 2) * inverse).astype(
        jnp.bfloat16
    )
    new_values = (
        lax.dynamic_slice_in_dim(keyvals, (kv_heads + head_group) * HD, HD, 2) * inverse
    ).astype(jnp.bfloat16)
    return (queries, new_keys, new_values)


def coarse_attention(queries, step_ids, cache_own, cache_len, key_store, value_store, mark_store):
    length = cache_own.shape[1]
    step_count = key_store.shape[1]
    scaling = HD ** (-0.5)
    scores_old = (
        jnp.einsum(
            "rbd,rld->rbl", queries, cache_own[:, :, :HD], preferred_element_type=jnp.float32
        )
        * scaling
    )
    valid_old = jnp.arange(length, dtype=jnp.int32)[None, :] < cache_len[:, None]
    scores_old = jnp.where(valid_old[:, None, :], scores_old, NEG_FILL)
    scores_new = (
        jnp.einsum("rbd,rud->rbu", queries, key_store, preferred_element_type=jnp.float32) * scaling
    )
    valid_new = (jnp.arange(step_count)[None, None, :] <= step_ids[None, :, None]) & (
        mark_store[:, None, :] > 0.5
    )
    scores_new = jnp.where(valid_new, scores_new, NEG_FILL)
    weights_old, weights_new = split_softmax(scores_old, scores_new)
    mixed_heads = jnp.einsum(
        "rbl,rld->rbd", weights_old, cache_own[:, :, HD:], preferred_element_type=jnp.float32
    )
    mixed_heads = mixed_heads + jnp.einsum(
        "rbu,rud->rbd", weights_new, value_store, preferred_element_type=jnp.float32
    )
    return mixed_heads.astype(jnp.bfloat16)


def give_back(mixed_heads, return_weight, owners, ranking):
    row_index = lax.axis_index("streams")
    column = lax.axis_index("tp")
    summed = lax.psum_scatter(
        jnp.einsum("rbh,hd->rbd", mixed_heads, return_weight, preferred_element_type=jnp.float32),
        "tp",
        scatter_dimension=0,
        tiled=True,
    ).astype(jnp.bfloat16)
    every_back = lax.all_gather(summed, "streams", axis=0, tiled=True)
    my_owner = lax.dynamic_index_in_dim(
        lax.dynamic_index_in_dim(owners, column, 0, keepdims=False), row_index, 0, keepdims=False
    )
    my_rank = lax.dynamic_index_in_dim(
        lax.dynamic_index_in_dim(ranking, column, 0, keepdims=False), row_index, 0, keepdims=False
    )
    return lax.dynamic_index_in_dim(every_back, my_owner * OWNED_MOST + my_rank, 0, keepdims=False)


def shards(
    hidden_in,
    byte_qkv,
    byte_cache,
    byte_len,
    flags,
    coarse_prev,
    owner_map,
    up_weight,
    coarse_gain,
    query_weight,
    keyval_weight,
    return_weight,
    coarse_cache,
    coarse_len,
):
    step_count = hidden_in.shape[1]
    attended = byte_attention(byte_qkv, byte_cache, byte_len)
    byte_rows = (hidden_in.astype(jnp.float32) + attended).astype(jnp.bfloat16)
    byte_marks = flags.astype(jnp.bfloat16)
    owners, ranking = rank_table(owner_map)
    cache_own = coarse_cache[0, :, 0]
    cache_len = coarse_len[0]
    slot_rows, slot_marks = dispatch(byte_rows, byte_marks, owners, ranking)
    queries, new_keys, new_values = coarse_project(
        slot_rows, up_weight, coarse_gain, query_weight, keyval_weight
    )
    step_ids = jnp.arange(step_count, dtype=jnp.int32)
    mixed_heads = coarse_attention(
        queries, step_ids, cache_own, cache_len, new_keys, new_values, slot_marks
    )
    given_back = give_back(mixed_heads, return_weight, owners, ranking)
    current = coarse_prev[0].astype(jnp.float32)
    outputs = []
    for step in range(step_count):
        current = jnp.where(flags[0, step] > 0, given_back[step].astype(jnp.float32), current)
        outputs.append(byte_rows[0, step].astype(jnp.float32) + current)
    return jnp.stack(outputs)[None].astype(jnp.bfloat16)


def solution(mesh):
    return jax.shard_map(
        shards,
        mesh=mesh,
        in_specs=(
            P(("streams", "tp"), None, None),
            P(("streams", "tp"), None, None),
            P(("streams", "tp"), None, None),
            P(("streams", "tp")),
            P(("streams", "tp"), None),
            P(("streams", "tp"), None),
            P(),
            P(None, "tp"),
            P(),
            P(None, "tp"),
            P("tp", None),
            P("tp", None),
            P("streams", None, "tp", None, None),
            P("streams", None),
        ),
        out_specs=P(("streams", "tp"), None, None),
        check_vma=False,
    )
```

profile of v0, /device:TPU:1, one launch (start us, length us, event | category | flops | bytes accessed | tf_op | source)
XLA Modules:
  0.0 587.4 jit_solution(7376833832583837293)
XLA Ops:
  6.6 1.1 fusion.96
  7.9 0.7 slice.62
  9.3 0.9 convolution_multiply_fusion.2
  10.2 0.2 fusion.98
  10.9 0.2 fusion.58
  11.1 0.9 fusion.32
  12.0 0.7 fusion.61
  12.7 0.6 copy.147
  13.4 0.9 convert_reduce_fusion
  14.3 0.7 select_bitcast_fusion
  15.1 122.9 %all-gather.4.cloned.1.call-done = bf16[512,4,1024]{2,1,0:T(4,128)(2,1)} async-done(((bf16[1,4,1024]{2,1,0:T(4,128)(2,1)}), bf16[512,4,1024]{2,1,0:T(4,128)(2,1)}) %all-gather.4.cloned.1.call-update) | async-done | bytes 4194320 | tf_op jit(solution)/shard_map/all_gather | solution.py:84
  138.0 5.7 fusion.14
  143.8 1.2 fusion.100
  145.1 0.6 dynamic_slice.27
  146.9 90.5 %all-gather = bf16[512,1,4]{2,1,0:T(2,128)(2,1)S(1)} all-gather(bf16[1,1,4]{2,1,0:T(2,128)(2,1)S(1)} %convert_bitcast_fusion), channel_id=1, replica_groups=mesh['streams'=16,'tp'=32] {'streams','tp'}, dimensions={0}, use_global_device_ids=true | all-gather | bytes 4104 | tf_op jit(solution)/shard_map/all_gather | solution.py:85
  237.6 0.7 fusion.97
  240.9 1.3 dynamic-slice.4
  243.1 2.2 fusion.35
  245.4 3.3 fusion.1
  248.8 1.2 fusion.23
  250.1 148.3 %all-reduce.4.cloned.1.call-done = f32[64,4,1024]{2,0,1:T(8,128)} async-done(((f32[64,4,1024]{2,0,1:T(8,128)}), f32[64,4,1024]{2,0,1:T(8,128)}) %all-reduce.4.cloned.1.call-update) | async-done | bytes 1048592 | tf_op jit(solution)/shard_map/psum | solution.py:127
  398.4 1.1 multiply_convert_fusion.2
  399.5 0.2 fusion.48
  400.0 1.5 fusion.99
  401.6 0.2 fusion.44
  402.5 1.4 fusion.28
  403.9 0.3 fusion.38
  404.2 0.7 copy.161
  404.9 125.0 %all-reduce.5 = bf16[64,4,1024]{2,1,0:T(4,128)(2,1)} all-reduce(f32[64,4,1024]{2,1,0:T(4,128)S(1)} %copy.161), channel_id=2, replica_groups=mesh['streams'=16,'tp'=32] {'tp'}, use_global_device_ids=true, to_apply=%region_11.12.clone | all-reduce | flops 262144 | bytes 1572864
  529.9 0.7 dynamic-slice_convert_fusion
  530.6 49.6 %all_gather.15 = bf16[32,4,1024]{2,1,0:T(4,128)(2,1)S(1)} all-gather(bf16[2,4,1024]{2,1,0:T(4,128)(2,1)S(1)} %dynamic-slice_convert_fusion), channel_id=1, replica_groups=mesh['streams'=16,'tp'=32] {'streams'}, dimensions={0}, use_global_device_ids=true | all-gather | bytes 278528 | tf_op jit(solution)/shard_map/all_gather | solution.py:175
  580.2 0.6 pad_maximum_fusion
  (59 shorter events, 2.7 us)
Async XLA Ops:
  6.5 242.1 %copy-start = (bf16[8192,128]{1,0:T(8,128)(2,1)S(1)}, bf16[8192,128]{1,0:T(8,128)(2,1)}, u32[]{:S(2)}) copy-start(bf16[8192,128]{1,0:T(8,128)(2,1)} %param.23) | copy-start | bytes 6291460
  6.5 140.4 %copy-start.4 = (s32[1,4]{1,0:T(1,128)S(1)}, s32[1,4]{1,0:T(1,128)}, u32[]{:S(2)}) copy-start(s32[1,4]{1,0:T(1,128)} %param.18) | copy-start | bytes 52
  6.5 131.5 %all-gather.4.cloned.1.call-start = ((), (), s32[]{:S(2)}) async-start(), calls=%async_computation | async-start | bytes 4202496 | tf_op jit(solution)/shard_map/all_gather | solution.py:84
  6.5 234.3 %copy-start.7 = (f32[8192]{0:T(1024)S(1)}, f32[8192]{0:T(1024)}, u32[]{:S(2)}) copy-start(f32[8192]{0:T(1024)} %param.22) | copy-start | bytes 98308
  6.6 236.4 %copy-start.6 = (s32[1,64]{1,0:T(1,128)S(1)}, s32[1,64]{1,0:T(1,128)}, u32[]{:S(2)}) copy-start(s32[1,64]{1,0:T(1,128)} %param.27) | copy-start | bytes 772
  6.6 236.5 %copy-start.2 = (bf16[256,1024]{1,0:T(8,128)(2,1)S(1)}, bf16[256,1024]{1,0:T(8,128)(2,1)}, u32[]{:S(2)}) copy-start(bf16[256,1024]{1,0:T(8,128)(2,1)} %param.24) | copy-start | bytes 1572868
  13.3 232.0 %all-gather.6.cloned.1.call-start = ((), (), s32[]{:S(2)}) async-start(), calls=%async_computation.1 | async-start | bytes 4325376 | tf_op jit(solution)/shard_map/all_gather | solution.py:109
  143.7 254.7 %all-reduce.4.cloned.1.call-start = ((), (), s32[]{:S(2)}) async-start(), calls=%async_computation.2 | async-start | bytes 2097152 | tf_op jit(solution)/shard_map/psum | solution.py:127
  245.4 3.5 copy-start.1
  250.1 153.9 %copy-start.3 = (bf16[128,1024]{1,0:T(8,128)(2,1)S(1)}, bf16[128,1024]{1,0:T(8,128)(2,1)}, u32[]{:S(2)}) copy-start(bf16[128,1024]{1,0:T(8,128)(2,1)} %param.25) | copy-start | bytes 786436
  401.5 178.7 %copy-start.5 = (bf16[1,1024]{1,0:T(2,128)(2,1)S(1)}, bf16[1,1024]{1,0:T(2,128)(2,1)}, u32[]{:S(2)}) copy-start(bf16[1,1024]{1,0:T(2,128)(2,1)} %param.19) | copy-start | bytes 6148
Sparse Core Ops, SparseCore 0:
  13.5 124.5 all-gather.3
  143.8 85.0 all-gather.5
  245.4 152.8 all-reduce.3
where the time goes:
time: 588 us; the launch traced here: 587 us
  waiting for transfers between devices  271 us (46%)
  blocking collectives  265 us (45%)
  between operations  18.6 us (3%)
  matrix products  15 us (3%)
  other arithmetic  9.66 us (2%)
  local copies, waits for them, and re-layouts  7.67 us (1%)
    psum x1, waiting for transfers between devices, coarse_project(): keyvals = lax.psum(keyval_part, 'tp')  148 us
    unnamed x1, blocking collectives  125 us
    all_gather x1, waiting for transfers between devices, dispatch(): lax.all_gather(block_rows, ('streams', 'tp'), axis=0, tiled=True)  123 us
    all_gather x1, blocking collectives, dispatch(): lax.all_gather(block_marks, ('streams', 'tp'), axis=0, tiled=True)  90.5 us
    all_gather x1, blocking collectives, give_back(): every_back = lax.all_gather(summed, 'streams', axis=0, tiled=True)  49.6 us
  transfers between devices with their start and end apart: 3, of which 2 were waited for; matrix products, arithmetic and copies ran while one was open for 2% of the time, Pallas kernels for 0%

commit v1 on v0

--- a/solution.py
+++ b/solution.py
@@ -1,3 +1,4 @@
+import functools
 import jax
 import jax.numpy as jnp
 from jax import lax
@@ -7,6 +8,19 @@
 OWNED_MOST = 2
 EPSILON = 1e-05
 NEG_FILL = -1e30
+
+
+def loops_press(unit, mesh_name):
+    b_now, front = (unit, 0)
+    sides = lax.axis_size(mesh_name)
+    while 1 << front < sides:
+        high = lax.ppermute(b_now, mesh_name, perm=[(s, s ^ 1 << front) for s in range(sides)])
+        b_now = b_now + high
+        front = front + 1
+    return b_now
+
+
+convert_point = functools.partial(loops_press, mesh_name="tp")
 
 
 def split_softmax(scores_old, scores_new):
@@ -124,7 +138,7 @@
     keyval_part = jnp.einsum(
         "rbf,fc->rbc", own_scaled, keyval_weight, preferred_element_type=jnp.float32
     )
-    keyvals = lax.psum(keyval_part, "tp")
+    keyvals = convert_point(keyval_part)
     new_keys = (lax.dynamic_slice_in_dim(keyvals, head_group * HD, HD, 2) * inverse).astype(
         jnp.bfloat16
     )

time: 588 us -> 619 us (1.053)
  starting transfers between devices: 0.09 us -> 17.4 us
  waiting for transfers between devices: 271 us -> 280 us
    ppermute x0 -> x5, waiting for transfers between devices: none -> 157 us  [loops_press(): lax.ppermute(b_now, mesh_name, perm=[(s, s ^ 1 << front) for s in range(s...]
    psum x1 -> x0, waiting for transfers between devices: 148 us -> none  [coarse_project(): keyvals = lax.psum(keyval_part, 'tp')]
    ppermute x0 -> x5, starting transfers between devices: none -> 17.3 us  [loops_press(): lax.ppermute(b_now, mesh_name, perm=[(s, s ^ 1 << front) for s in range(s...]
    all_gather x1, blocking collectives: 90.5 us -> 101 us  [dispatch(): lax.all_gather(block_marks, ('streams', 'tp'), axis=0, tiled=True)]
    all_gather x1, blocking collectives: 49.6 us -> 43.2 us  [give_back(): every_back = lax.all_gather(summed, 'streams', axis=0, tiled=True)]
  transfers between devices with their start and end apart: 3 -> 7, of which waited for: 2 -> 5; matrix products, arithmetic and copies ran while one was open for 2% -> 2% of each run, Pallas kernels for 0% -> 0%
where the time goes in v1:
time: 619 us; the launch traced here: 618 us
  waiting for transfers between devices  280 us (45%)
  blocking collectives  268 us (43%)
  between operations  19 us (3%)
  starting transfers between devices  17.4 us (3%)
  matrix products  14 us (2%)
  other arithmetic  12.7 us (2%)
  local copies, waits for them, and re-layouts  7.53 us (1%)
    ppermute x5, waiting for transfers between devices, loops_press(): lax.ppermute(b_now, mesh_name, perm=[(s, s ^ 1 << front) for s in range(s...  157 us
    unnamed x1, blocking collectives  123 us
    all_gather x1, waiting for transfers between devices, dispatch(): lax.all_gather(block_rows, ('streams', 'tp'), axis=0, tiled=True)  123 us
    all_gather x1, blocking collectives, dispatch(): lax.all_gather(block_marks, ('streams', 'tp'), axis=0, tiled=True)  101 us
    all_gather x1, blocking collectives, give_back(): every_back = lax.all_gather(summed, 'streams', axis=0, tiled=True)  43.2 us
    ppermute x5, starting transfers between devices, loops_press(): lax.ppermute(b_now, mesh_name, perm=[(s, s ^ 1 << front) for s in range(s...  17.3 us
  transfers between devices with their start and end apart: 7, of which 5 were waited for; matrix products, arithmetic and copies ran while one was open for 2% of the time, Pallas kernels for 0%

profile of v1, /device:TPU:1, one launch (start us, length us, event | category | flops | bytes accessed | tf_op | source)
XLA Modules:
  0.0 618.2 jit_solution(16436530492811540680)
XLA Ops:
  6.6 1.1 fusion.96
  7.9 0.7 slice.62
  9.3 0.9 convolution_multiply_fusion.2
  11.1 0.9 fusion.32
  12.0 0.7 fusion.61
  13.4 0.9 convert_reduce_fusion
  14.3 0.7 select_bitcast_fusion
  15.1 122.9 %all-gather.4.cloned.1.call-done = bf16[512,4,1024]{2,1,0:T(4,128)(2,1)} async-done(((bf16[1,4,1024]{2,1,0:T(4,128)(2,1)}), bf16[512,4,1024]{2,1,0:T(4,128)(2,1)}) %all-gather.4.cloned.1.call-update) | async-done | bytes 4194320 | tf_op jit(solution)/shard_map/all_gather | solution.py:98
  138.0 5.7 fusion.14
  143.8 1.2 fusion.35
  145.0 2.5 collective-permute-start
  147.5 26.9 %collective-permute-done = f32[64,4,1024]{2,0,1:T(8,128)S(1)} collective-permute-done((f32[64,4,1024]{2,0,1:T(8,128)S(1)}, f32[64,4,1024]{2,0,1:T(8,128)S(1)}, u32[]{:S(2)}, u32[]{:S(2)}) %collective-permute-start) | collective-permute-done | bytes 1048608 | tf_op jit(solution)/shard_map/ppermute | solution.py:17
  174.6 2.4 collective-permute-start.1
  177.0 48.2 %collective-permute-done.1 = f32[64,4,1024]{2,0,1:T(8,128)S(1)} collective-permute-done((f32[64,4,1024]{2,0,1:T(8,128)S(1)}, f32[64,4,1024]{2,0,1:T(8,128)S(1)}, u32[]{:S(2)}, u32[]{:S(2)}) %collective-permute-start.1) | collective-permute-done | bytes 1048608 | tf_op jit(solution)/shard_map/ppermute | solution.py:17
  225.4 5.6 collective-permute-start.2
  231.1 59.6 %collective-permute-done.2 = f32[64,4,1024]{2,0,1:T(8,128)S(1)} collective-permute-done((f32[64,4,1024]{2,0,1:T(8,128)S(1)}, f32[64,4,1024]{2,0,1:T(8,128)S(1)}, u32[]{:S(2)}, u32[]{:S(2)}) %collective-permute-start.2) | collective-permute-done | bytes 1048608 | tf_op jit(solution)/shard_map/ppermute | solution.py:17
  290.8 1.9 collective-permute-start.3
  292.8 22.0 %collective-permute-done.3 = f32[64,4,1024]{2,0,1:T(8,128)S(1)} collective-permute-done((f32[64,4,1024]{2,0,1:T(8,128)S(1)}, f32[64,4,1024]{2,0,1:T(8,128)S(1)}, u32[]{:S(2)}, u32[]{:S(2)}) %collective-permute-start.3) | collective-permute-done | bytes 1048608 | tf_op jit(solution)/shard_map/ppermute | solution.py:17
  314.9 5.0 collective-permute-start.4
  319.9 1.2 fusion.100
  323.1 101.1 %all-gather = bf16[512,1,4]{2,1,0:T(2,128)(2,1)S(1)} all-gather(bf16[1,1,4]{2,1,0:T(2,128)(2,1)S(1)} %convert_bitcast_fusion), channel_id=1, replica_groups=mesh['streams'=16,'tp'=32] {'streams','tp'}, dimensions={0}, use_global_device_ids=true | all-gather | bytes 4104 | tf_op jit(solution)/shard_map/all_gather | solution.py:99
  427.6 1.3 dynamic-slice.4
  429.8 2.4 add.132
  432.2 3.3 fusion.1
  435.4 1.1 multiply_convert_fusion.2
  436.5 1.2 fusion.23
  438.3 1.5 fusion.99
  440.9 1.4 fusion.28
  442.6 0.7 copy.161
  443.2 123.5 %all-reduce.2 = bf16[64,4,1024]{2,1,0:T(4,128)(2,1)} all-reduce(f32[64,4,1024]{2,1,0:T(4,128)S(1)} %copy.161), channel_id=2, replica_groups=mesh['streams'=16,'tp'=32] {'tp'}, use_global_device_ids=true, to_apply=%region_10.11.clone | all-reduce | flops 262144 | bytes 1572864
  566.7 0.7 dynamic-slice_convert_fusion
  567.4 43.2 %all_gather.15 = bf16[32,4,1024]{2,1,0:T(4,128)(2,1)S(1)} all-gather(bf16[2,4,1024]{2,1,0:T(4,128)(2,1)S(1)} %dynamic-slice_convert_fusion), channel_id=1, replica_groups=mesh['streams'=16,'tp'=32] {'streams'}, dimensions={0}, use_global_device_ids=true | all-gather | bytes 278528 | tf_op jit(solution)/shard_map/all_gather | solution.py:189
  (71 shorter events, 6.8 us)
Async XLA Ops:
  6.5 430.0 %copy-start = (bf16[8192,128]{1,0:T(8,128)(2,1)S(1)}, bf16[8192,128]{1,0:T(8,128)(2,1)}, u32[]{:S(2)}) copy-start(bf16[8192,128]{1,0:T(8,128)(2,1)} %param.23) | copy-start | bytes 6291460
  6.5 137.2 %copy-start.7 = (f32[8192]{0:T(1024)S(1)}, f32[8192]{0:T(1024)}, u32[]{:S(2)}) copy-start(f32[8192]{0:T(1024)} %param.22) | copy-start | bytes 98308
  6.5 137.2 %copy-start.2 = (bf16[256,1024]{1,0:T(8,128)(2,1)S(1)}, bf16[256,1024]{1,0:T(8,128)(2,1)}, u32[]{:S(2)}) copy-start(bf16[256,1024]{1,0:T(8,128)(2,1)} %param.24) | copy-start | bytes 1572868
  6.5 131.5 %all-gather.4.cloned.1.call-start = ((), (), s32[]{:S(2)}) async-start(), calls=%async_computation | async-start | bytes 4202496 | tf_op jit(solution)/shard_map/all_gather | solution.py:98
  13.3 418.9 %all-gather.6.cloned.1.call-start = ((), (), s32[]{:S(2)}) async-start(), calls=%async_computation.1 | async-start | bytes 4325376 | tf_op jit(solution)/shard_map/all_gather | solution.py:123
  145.0 29.4 %collective-permute-start = (f32[64,4,1024]{2,0,1:T(8,128)S(1)}, f32[64,4,1024]{2,0,1:T(8,128)S(1)}, u32[]{:S(2)}, u32[]{:S(2)}) collective-permute-start(f32[64,4,1024]{2,0,1:T(8,128)S(1)} %fusion.35), channel_id=1, source_target_pairs={{0,1},{1,0},{2,3},{3,2},{4,5},{5,4},{6,7},{7,6},{8,9},{9,8},{10,11... | collective-permute-start | bytes 3145736 | tf_op jit(solution)/shard_map/ppermute | solution.py:17
  174.6 148.4 %copy-start.4 = (s32[1,4]{1,0:T(1,128)S(1)}, s32[1,4]{1,0:T(1,128)}, u32[]{:S(2)}) copy-start(s32[1,4]{1,0:T(1,128)} %param.18) | copy-start | bytes 52
  174.6 50.6 %collective-permute-start.1 = (f32[64,4,1024]{2,0,1:T(8,128)S(1)}, f32[64,4,1024]{2,0,1:T(8,128)S(1)}, u32[]{:S(2)}, u32[]{:S(2)}) collective-permute-start(f32[64,4,1024]{2,0,1:T(8,128)S(1)} %add.128), channel_id=1, source_target_pairs={{0,2},{1,3},{2,0},{3,1},{4,6},{5,7},{6,4},{7,5},{8,10},{9,11},{10,... | collective-permute-start | bytes 3145736 | tf_op jit(solution)/shard_map/ppermute | solution.py:17
  225.4 204.2 %copy-start.6 = (s32[1,64]{1,0:T(1,128)S(1)}, s32[1,64]{1,0:T(1,128)}, u32[]{:S(2)}) copy-start(s32[1,64]{1,0:T(1,128)} %param.27) | copy-start | bytes 772
  225.4 65.2 %collective-permute-start.2 = (f32[64,4,1024]{2,0,1:T(8,128)S(1)}, f32[64,4,1024]{2,0,1:T(8,128)S(1)}, u32[]{:S(2)}, u32[]{:S(2)}) collective-permute-start(f32[64,4,1024]{2,0,1:T(8,128)S(1)} %add.129), channel_id=1, source_target_pairs={{0,4},{1,5},{2,6},{3,7},{4,0},{5,1},{6,2},{7,3},{8,12},{9,13},{10,... | collective-permute-start | bytes 3145736 | tf_op jit(solution)/shard_map/ppermute | solution.py:17
  290.8 23.9 %collective-permute-start.3 = (f32[64,4,1024]{2,0,1:T(8,128)S(1)}, f32[64,4,1024]{2,0,1:T(8,128)S(1)}, u32[]{:S(2)}, u32[]{:S(2)}) collective-permute-start(f32[64,4,1024]{2,0,1:T(8,128)S(1)} %add.130), channel_id=1, source_target_pairs={{0,8},{1,9},{2,10},{3,11},{4,12},{5,13},{6,14},{7,15},{8,0},{9,1},... | collective-permute-start | bytes 3145736 | tf_op jit(solution)/shard_map/ppermute | solution.py:17
  314.9 114.8 %collective-permute-start.4 = (f32[64,4,1024]{2,0,1:T(8,128)S(1)}, f32[64,4,1024]{2,0,1:T(8,128)}, u32[]{:S(2)}, u32[]{:S(2)}) collective-permute-start(f32[64,4,1024]{2,0,1:T(8,128)S(1)} %add.131), channel_id=1, source_target_pairs={{0,16},{1,17},{2,18},{3,19},{4,20},{5,21},{6,22},{7,23},{8,24},{9,... | collective-permute-start | bytes 3145736 | tf_op jit(solution)/shard_map/ppermute | solution.py:17
  432.2 4.4 copy-start.1
  436.5 5.7 copy-start.3
  439.8 170.9 %copy-start.5 = (bf16[1,1024]{1,0:T(2,128)(2,1)S(1)}, bf16[1,1024]{1,0:T(2,128)(2,1)}, u32[]{:S(2)}) copy-start(bf16[1,1024]{1,0:T(2,128)(2,1)} %param.19) | copy-start | bytes 6148
Sparse Core Ops, SparseCore 0:
  13.4 124.5 all-gather.3
  143.8 161.3 all-gather.5
